TPU v7x, 768 devices: a whole 4x8x12 slice. The times are simulated.
768 devices in a mesh: row: 16 (over y, core), col: 4 (over x), depth: 12 (over z).
Axes of the slice: x: 4, y: 8, z: 12, core: 2. Of those that a mesh axis runs over, the one named last changes fastest.
Arguments:
- row_stripe: bfloat16 [1920, 12, 8704], P('row', 'depth', 'col'), may hold values from -0.01953125 to 0.01953125
- column_stripe: bfloat16 [12, 8704, 1920], P('depth', 'row', 'col'), may hold values from -9 to 9
- window_block: bfloat16 [1920, 1920], P('row', ('col', 'depth')), may hold values from -3 to 3
- stripe_tiles: int32 [15, 816], replicated, may hold values 0 or 1
- column_tiles: int32 [816, 15], replicated, may hold values 0 or 1
- keep_tiles: int32 [15, 15], replicated, may hold values 0 or 1
- branch: int32 [15], replicated, may hold values from 0 to 1
Outputs:
- new_block: bfloat16 [1920, 1920], P('row', ('col', 'depth'))
- occupancy: float32 [], replicated
All inputs are finite; a program needn't handle non-finite values.
Results may differ from a plain program's by a relative error of at most 0.0018.
Values may be sent and summed in bfloat16 or wider, within the bound.
A program may use at most 32 MiB of HBM per device.

v0:
```python
import jax
import jax.numpy as jnp
from jax import lax
from jax.sharding import PartitionSpec as P

TILE = 128


def expand(table, row_start, row_count, col_start, col_count):
    tile_rows = row_count // TILE + 2
    tile_cols = col_count // TILE + 2
    padded = jnp.pad(table > 0, ((0, tile_rows), (0, tile_cols)))
    tile_block = lax.dynamic_slice(
        padded, (row_start // TILE, col_start // TILE), (tile_rows, tile_cols)
    )
    expanded = jnp.repeat(jnp.repeat(tile_block, TILE, axis=0), TILE, axis=1)
    return lax.dynamic_slice(expanded, (row_start % TILE, col_start % TILE), (row_count, col_count))


def shards(row_stripe, column_stripe, window_block, stripe_tiles, column_tiles, keep_tiles, branch):
    row_count = row_stripe.shape[0]
    left_width = row_stripe.shape[2]
    right_height = column_stripe.shape[1]
    col_count = column_stripe.shape[2]
    layer_width = left_width * lax.axis_size("col")
    row_pos = lax.axis_index("row")
    col_pos = lax.axis_index("col")
    depth_pos = lax.axis_index("depth")
    layer_start = depth_pos * layer_width
    left_mask = expand(
        stripe_tiles, row_pos * row_count, row_count, layer_start + col_pos * left_width, left_width
    )
    left_rows = jnp.where(left_mask, row_stripe[:, 0, :], jnp.zeros((), jnp.bfloat16))
    right_mask = expand(
        column_tiles,
        layer_start + row_pos * right_height,
        right_height,
        col_pos * col_count,
        col_count,
    )
    right_cols = jnp.where(right_mask, column_stripe[0], jnp.zeros((), jnp.bfloat16))
    squared = left_rows.astype(jnp.float32)
    own_term = jnp.sum(squared * squared)
    wide_left = lax.all_gather(left_rows, "col", axis=1, tiled=True)
    partial_sum = jnp.dot(
        wide_left,
        lax.all_gather(right_cols, "row", axis=0, tiled=True),
        preferred_element_type=jnp.float32,
    )
    occupancy = lax.psum(own_term, ("row", "col", "depth"))
    square = lax.psum_scatter(partial_sum, "depth", scatter_dimension=1, tiled=True)
    occupancy = occupancy / (row_count * lax.axis_size("row"))
    out_cols = square.shape[1]
    keep_mask = expand(
        keep_tiles,
        row_pos * row_count,
        row_count,
        col_pos * col_count + depth_pos * out_cols,
        out_cols,
    )
    branch_rows = expand(branch[:, None], row_pos * row_count, row_count, 0, 1)
    doubled = 2.0 * window_block.astype(jnp.float32) - square
    updated = jnp.where(branch_rows, doubled, square)
    new_block = jnp.where(keep_mask, updated, jnp.zeros((), jnp.float32)).astype(jnp.bfloat16)
    return (new_block, occupancy)


def solution(mesh):
    return jax.shard_map(
        shards,
        mesh=mesh,
        in_specs=(
            P("row", "depth", "col"),
            P("depth", "row", "col"),
            P("row", ("col", "depth")),
            P(),
            P(),
            P(),
            P(),
        ),
        out_specs=(P("row", ("col", "depth")), P()),
        check_vma=False,
    )
```

profile of v0, /device:TPU:1, one launch (start us, length us, event | category | flops | bytes accessed | tf_op | source)
XLA Modules:
  0.0 255.4 jit_solution(316118132405544157)
XLA Ops:
  7.3 0.9 broadcast_compare_fusion.1
  8.2 0.1 pad_dynamic-slice_fusion.1
  8.3 0.1 copy.20
  8.4 0.1 broadcast_bitcast_fusion
  8.6 1.4 copy.21
  10.0 0.2 broadcast_in_dim.54
  10.1 1.9 multiply_reduce_fusion
  12.2 0.1 pad_dynamic-slice_fusion
  12.3 0.1 broadcast_bitcast_fusion.1
  12.5 0.3 copy.22
  12.8 0.1 broadcast_in_dim.57
  12.9 0.4 dynamic-slice_select_fusion
  13.3 1.1 copy.23
  14.5 0.1 pad_dynamic-slice_fusion.2
  14.6 0.1 copy.19
  14.7 0.1 broadcast_bitcast_fusion.3
  14.8 45.0 %all-gather.3.cloned.1.call-done = bf16[120,8704]{0,1:T(8,128)(2,1)} async-done(((bf16[120,2176]{0,1:T(8,128)(2,1)}), bf16[120,8704]{0,1:T(8,128)(2,1)}) %all-gather.3.cloned.1.call-update) | async-done | bytes 2088976 | tf_op jit(solution)/shard_map/all_gather | solution.py:44
  59.8 66.4 %all-gather.5.cloned.1.call-done = bf16[8704,480]{1,0:T(8,128)(2,1)} async-done(((bf16[544,480]{1,0:T(8,128)(2,1)}), bf16[8704,480]{1,0:T(8,128)(2,1)}) %all-gather.5.cloned.1.call-update) | async-done | bytes 8355856 | tf_op jit(solution)/shard_map/all_gather | solution.py:47
  126.2 8.4 %fusion.2 = f32[120,480]{0,1:T(8,128)} fusion(bf16[120,8704]{0,1:T(8,128)(2,1)} %all-gather.3.cloned.1.call-done, bf16[8704,480]{1,0:T(8,128)(2,1)} %all-gather.5.cloned.1.call-done), kind=kOutput, calls=%fused_computation.22 | convolution fusion | flops 1002700800 | bytes 10675200 | tf_op jit(solution)/shard_map/dot_general | solution.py:45
  134.7 110.6 %psum.7 = f32[]{:T(128)} all-reduce(f32[]{:T(128)} %get-tuple-element.2), channel_id=1, replica_groups=mesh['row'=16,'col'=4,'depth'=12] {'row','col','depth'}, use_global_device_ids=true, to_apply=%region_2.3 | all-reduce | flops 1 | bytes 8 | tf_op jit(solution)/shard_map/psum | solution.py:50
  245.3 0.1 pad_dynamic-slice_fusion.3
  245.4 0.1 broadcast_bitcast_fusion.2
  246.2 0.1 dynamic-slice_bitcast_fusion
  246.3 1.4 fusion.1
  (27 shorter events, 0.3 us)
Async XLA Ops:
  7.2 5.0 %copy-start.1 = (s32[816,15]{0,1:T(8,128)S(1)}, s32[816,15]{0,1:T(8,128)}, u32[]{:S(2)}) copy-start(s32[816,15]{0,1:T(8,128)} %param.11) | copy-start | bytes 146884
  7.2 5.3 %copy-start = (bf16[1,544,480]{2,1,0:T(8,128)(2,1)S(1)}, bf16[1,544,480]{2,1,0:T(8,128)(2,1)}, u32[]{:S(2)}) copy-start(bf16[1,544,480]{2,1,0:T(8,128)(2,1)} %param.8) | copy-start | bytes 1566724
  7.2 52.6 %all-gather.3.cloned.1.call-start = ((), (), s32[]{:S(2)}) async-start(), calls=%async_computation.1 | async-start | bytes 2785280 | tf_op jit(solution)/shard_map/all_gather | solution.py:44
  12.1 114.1 %all-gather.5.cloned.1.call-start = ((), (), s32[]{:S(2)}) async-start(), calls=%async_computation.2 | async-start | bytes 9469952 | tf_op jit(solution)/shard_map/all_gather | solution.py:47
  12.5 2.0 copy-start.3
  14.4 231.8 %reduce-scatter.4.cloned.1.call-start = ((), (), s32[]{:S(2)}) async-start(), calls=%async_computation.3 | async-start | bytes 266240
  14.8 119.8 %copy-start.4 = (s32[15]{0:T(128)S(1)}, s32[15]{0:T(128)}, u32[]{:S(2)}) copy-start(s32[15]{0:T(128)} %param.13) | copy-start | bytes 184
  14.8 231.5 %copy-start.2 = (bf16[120,40]{0,1:T(8,128)(2,1)S(1)}, bf16[120,40]{0,1:T(8,128)(2,1)}, u32[]{:S(2)}) copy-start(bf16[120,40]{0,1:T(8,128)(2,1)} %param.9) | copy-start | bytes 28804
Sparse Core Ops, SparseCore 0:
  12.2 47.5 all-gather.2
  62.2 63.9 all-gather.4
  134.8 47.3 reduce-scatter.3
where the time goes:
time: 256 us; the launch traced here: 255 us
  waiting for transfers between devices  111 us (43%)
  blocking collectives  111 us (43%)
  between operations  15.9 us (6%)
  matrix products  8.41 us (3%)
  other arithmetic  4.66 us (2%)
  local copies, waits for them, and re-layouts  4.16 us (2%)
    psum x1, blocking collectives, shards(): occupancy = lax.psum(own_term, ('row', 'col', 'depth'))  111 us
    all_gather x1, waiting for transfers between devices, shards(): lax.all_gather(right_cols, 'row', axis=0, tiled=True)  66.4 us
    all_gather x1, waiting for transfers between devices, shards(): wide_left = lax.all_gather(left_rows, 'col', axis=1, tiled=True)  45 us
    dot_general x1, matrix products, shards(): jnp.dot(wide_left, lax.all_gather(right_cols, 'row', axis=0, tiled=True),...  8.41 us
  transfers between devices with their start and end apart: 3, of which 2 were waited for; matrix products, arithmetic and copies ran while one was open for 1% of the time, Pallas kernels for 0%

commit v1 on v0

v1 whole, which is shorter than its diff:
```python
import functools

import jax
import jax.numpy as jnp
from jax import lax
from jax.experimental import pallas as pl
from jax.experimental.pallas import tpu as pltpu
from jax.sharding import PartitionSpec as P

TILE = 128
MESH = pl.DeviceIdType.MESH
X, Y, Z = 4, 8, 12
ROWS = 120
ROWS_P = 128
PANEL = 2176
SUB = 544
COLS = 480
OUT = 40
KWIN = 1152
EARLY = 1


def segments(tile):
    found = []
    for z in range(Z):
        low = max(tile * TILE, z * OUT)
        high = min(tile * TILE + TILE, COLS, z * OUT + OUT)
        if low < high:
            found.append((z, low - tile * TILE, high - low, low - z * OUT))
    return found


def one_hot(hit):
    return jnp.where(hit, 1.0, 0.0).astype(jnp.bfloat16)


def dot(a, b):
    return jnp.dot(a, b, preferred_element_type=jnp.float32)


def kernel(
    row_ref, col_ref, win_ref, stripe_ref, ctab_ref, keep_ref, branch_ref,
    out_ref, occ_ref,
    rm, rb, lg, acc, ct, zin, occx, occy, occc, occz, keepm, branchm,
    rsend, rrecv, dsend, drecv, own_sem, lsend, lrecv, lsibs, lsibr, zsend, zrecv, osend, orecv,
):
    r = lax.axis_index("row")
    x = lax.axis_index("col")
    z = lax.axis_index("depth")
    y = r // 2
    c = r % 2

    def ydev(d):
        return (((y + d) % Y) * 2 + c, x, z)

    def xdev(d):
        return (r, (x + d) % X, z)

    sib = (y * 2 + (1 - c), x, z)

    barrier = pltpu.get_barrier_semaphore()
    peers = [ydev(d) for d in range(1, Y)] + [xdev(d) for d in range(1, X)] + [sib]
    for d in range(1, Z):
        peers.append((r, x, (z + d) % Z))
        peers.append((y * 2 + (1 - c), x, (z + d) % Z))
    for peer in peers:
        pl.semaphore_signal(barrier, inc=1, device_id=peer, device_id_type=MESH)

    for t in range(2):
        for yy in range(Y):
            low = 0 if yy % 2 else 2 * SUB
            rb[t, yy, low : low + 64, :] = jnp.zeros((64, TILE), jnp.bfloat16)

    first = z * 68 + (r * SUB) // TILE
    skew = (r * SUB) % TILE
    ctab = one_hot(ctab_ref[...] > 0)
    pick = one_hot(
        lax.broadcasted_iota(jnp.int32, (16, 816), 1)
        == lax.broadcasted_iota(jnp.int32, (16, 816), 0) + first
    )
    picked = dot(pick, ctab).astype(jnp.bfloat16)
    spread = one_hot(
        lax.broadcasted_iota(jnp.int32, (15, 512), 0)
        == (lax.broadcasted_iota(jnp.int32, (15, 512), 1) + x * COLS) // TILE
    )
    by_col = dot(picked, spread).astype(jnp.bfloat16)
    band = one_hot(
        lax.broadcasted_iota(jnp.int32, (SUB, 16), 1)
        == (lax.broadcasted_iota(jnp.int32, (SUB, 16), 0) + skew) // TILE
    )
    rm[3] = jnp.zeros((SUB, TILE), jnp.bfloat16)
    for tile in range(4):
        wide = min(TILE, COLS - tile * TILE)
        mask = dot(band, by_col[:, tile * TILE : tile * TILE + wide]).astype(jnp.bfloat16)
        rm[tile, :, 0:wide] = col_ref[0, :, tile * TILE : tile * TILE + wide] * mask

    pl.semaphore_wait(barrier, len(peers))

    def off(yy, cc):
        return pl.multiple_of((yy % 2) * 64 + cc * SUB, 32)

    def piece(t, yy, cc):
        return rb.at[t, yy, pl.ds(off(yy, cc), SUB), :]

    def which(d, k):
        if k == 6:
            return c if d > 0 else 1 - c
        return c if k % 2 == 0 else 1 - c

    def sent(d, t, k):
        yy = (y - d * (k // 2) + Y) % Y
        there = piece(t, yy, which(d, k))
        here = rm.at[2 * c + t] if k == 0 else there
        i = (0 if d > 0 else 14) + t * 7 + k
        return pltpu.make_async_remote_copy(
            src_ref=here, dst_ref=there, send_sem=rsend.at[i], recv_sem=rrecv.at[i],
            device_id=ydev(d % Y), device_id_type=MESH,
        )

    def got(d, t, k):
        yy = (y - d * (k // 2 + 1) + Y) % Y
        here = piece(t, yy, which(d, k))
        i = (0 if d > 0 else 14) + t * 7 + k
        return pltpu.make_async_copy(here, here, rrecv.at[i])

    ways = (1, -1)
    for d in ways:
        sent(d, 0, 0).start()

    def swap(t):
        return pltpu.make_async_remote_copy(
            src_ref=rm.at[2 * (1 - c) + t], dst_ref=piece(t, y, c),
            send_sem=dsend.at[t], recv_sem=drecv.at[t], device_id=sib, device_id_type=MESH,
        )

    def keep_own(t):
        return pltpu.make_async_copy(rm.at[2 * c + t], piece(t, y, c), own_sem.at[t])

    def swapped(t):
        here = piece(t, y, 1 - c)
        return pltpu.make_async_copy(here, here, drecv.at[t])

    for t in range(2):
        swap(t).start()
        keep_own(t).start()

    stab = one_hot(stripe_ref[...] > 0)
    base = z * 68 + x * 17
    shift = one_hot(
        lax.broadcasted_iota(jnp.int32, (816, TILE), 0)
        == lax.broadcasted_iota(jnp.int32, (816, TILE), 1) + base
    )
    narrow = dot(stab, shift).astype(jnp.bfloat16)
    rows_in = one_hot(
        lax.broadcasted_iota(jnp.int32, (ROWS, 15), 1)
        == (lax.broadcasted_iota(jnp.int32, (ROWS, 15), 0) + r * ROWS) // TILE
    )
    lmask = dot(rows_in, narrow)
    total = jnp.zeros((8, TILE), jnp.float32)
    myrow = pl.multiple_of(c * ROWS_P, ROWS_P)
    for k in range(17):
        part = row_ref[:, 0, k * TILE : k * TILE + TILE].astype(jnp.float32)
        part = part * lmask[:, k : k + 1]
        total = total + jnp.sum((part * part).reshape(15, 8, TILE), axis=0)
        whole = jnp.concatenate([part, jnp.zeros((8, TILE), jnp.float32)], axis=0)
        lg[x, pl.ds(myrow, ROWS_P), k * TILE : k * TILE + TILE] = whole.astype(jnp.bfloat16)
    occx[x] = total

    def half(panel, low):
        return lg.at[panel, pl.ds(pl.multiple_of(myrow + low, 64), 64), :]

    def lowrow(d, k):
        ahead = 0 if d > 0 else 64
        return 64 - ahead if k == 1 else ahead

    def lindex(d, k):
        return (0 if d > 0 else 3) + k

    def lsent(d, k):
        panel = (x - d + X) % X if k == 2 else x
        ref = half(panel, lowrow(d, k))
        return pltpu.make_async_remote_copy(
            src_ref=ref, dst_ref=ref, send_sem=lsend.at[lindex(d, k)],
            recv_sem=lrecv.at[lindex(d, k)], device_id=xdev(d % X), device_id_type=MESH,
        )

    def lpart(d, k):
        panel = (x - (2 * d if k == 2 else d) + X) % X
        return half(panel, lowrow(d, k))

    def lgot(d, k):
        here = lpart(d, k)
        return pltpu.make_async_copy(here, here, lrecv.at[lindex(d, k)])

    def lshare(d, k):
        ref = lpart(d, k)
        return pltpu.make_async_remote_copy(
            src_ref=ref, dst_ref=ref, send_sem=lsibs.at[lindex(d, k)],
            recv_sem=lsibr.at[lindex(d, k)], device_id=sib, device_id_type=MESH,
        )

    otherrow = pl.multiple_of((1 - c) * ROWS_P, ROWS_P)

    def lshared(d, k):
        panel = (x - (2 * d if k == 2 else d) + X) % X
        here = lg.at[panel, pl.ds(pl.multiple_of(otherrow + lowrow(d, k), 64), 64), :]
        return pltpu.make_async_copy(here, here, lsibr.at[lindex(d, k)])

    mine = lg.at[x, pl.ds(myrow, ROWS_P), :]
    share_own = pltpu.make_async_remote_copy(
        src_ref=mine, dst_ref=mine, send_sem=lsibs.at[6], recv_sem=lsibr.at[6],
        device_id=sib, device_id_type=MESH,
    )

    for k in range(2):
        for d in ways:
            lsent(d, k).start()
    share_own.start()

    swapped(0).wait()
    for d in ways:
        sent(d, 0, 1).start()
    swapped(1).wait()
    for k in range(EARLY):
        for d in ways:
            sent(d, 1, k).start()

    def osent(stage, i, buf, slot, device):
        return pltpu.make_async_remote_copy(
            src_ref=buf.at[slot], dst_ref=buf.at[slot], send_sem=osend.at[i],
            recv_sem=orecv.at[stage], device_id=device, device_id_type=MESH,
        )

    stage_sends = [
        [osent(0, d - 1, occx, x, xdev(d)) for d in range(1, X)],
        [osent(1, 2 + d, occy, y, ydev(d)) for d in range(1, Y)],
        [osent(2, 10, occc, c, sib)],
        [osent(3, 10 + d, occz, z, (r, x, (z + d) % Z)) for d in range(1, Z)],
    ]

    def ogot(stage, buf, n):
        here = buf.at[pl.ds(0, n)]
        pltpu.make_async_copy(here, here, orecv.at[stage]).wait()

    for copy in stage_sends[0]:
        copy.start()

    tabk = one_hot(keep_ref[...] > 0)
    cols_in = one_hot(
        lax.broadcasted_iota(jnp.int32, (15, TILE), 0)
        == (lax.broadcasted_iota(jnp.int32, (15, TILE), 1) + x * COLS + z * OUT) // TILE
    )
    keepm[...] = dot(rows_in, dot(tabk, cols_in).astype(jnp.bfloat16))
    flag = jnp.where(branch_ref[...] > 0, 1.0, 0.0)
    branchm[...] = jnp.broadcast_to(
        jnp.sum(rows_in.astype(jnp.float32) * flag, axis=1, keepdims=True), (ROWS, TILE)
    )

    def multiply(t, step, begin=False):
        yy = (y + step + Y) % Y
        window = pl.multiple_of((yy % 2) * 1024, 1024)
        product = dot(lg[yy // 2, :, pl.ds(window, KWIN)], rb[t, yy])
        if begin:
            acc[t] = product
        else:
            acc[t] += product

    def scatter(t, run):
        for n in range(2):

            @pl.when(c == n)
            def _():
                i = t * 8
                for zd, low, rows, at in segments(2 * n + t):
                    for cd in range(2):
                        src = ct.at[t, cd, pl.ds(low, rows), :]
                        dst = zin.at[z, pl.ds(at, rows), :]
                        far = pltpu.make_async_remote_copy(
                            src_ref=src, dst_ref=dst, send_sem=zsend.at[i], recv_sem=zrecv.at[0],
                            device_id=(y * 2 + cd, x, jnp.int32(zd)), device_id_type=MESH,
                        )
                        if cd == n:

                            @pl.when(z != zd)
                            def _():
                                far.start() if run else far.wait_send()

                            if run:

                                @pl.when(z == zd)
                                def _():
                                    pltpu.make_async_copy(src, dst, zrecv.at[0]).start()
                        else:
                            far.start() if run else far.wait_send()
                        i += 1

    def turn(t):
        for cd in range(2):
            ct[t, cd] = acc[t, cd * TILE : cd * TILE + TILE, :].T

    for t in range(2):
        for k in range(7):
            for d in ways:
                got(d, t, k).wait()
                if k < 4:
                    sent(d, t, k + 2).start()
                if k == (4 if d > 0 else 5):
                    sent(d, t, 6).start()
                if t == 0 and k == 4:
                    for j in range(EARLY, 2):
                        sent(d, 1, j).start()
            if (t, k) == (0, 1):
                for d in ways:
                    lgot(d, 0).wait()
                    lsent(d, 2).start()
                    lshare(d, 0).start()
            if (t, k) == (0, 2):
                ogot(0, occx, X - 1)
                occy[y] = occx[0] + occx[1] + occx[2] + occx[3]
                for copy in stage_sends[1]:
                    copy.start()
            if (t, k) == (0, 4):
                for d in ways:
                    lgot(d, 1).wait()
                    lshare(d, 1).start()
            if (t, k) == (0, 5):
                ogot(1, occy, Y - 1)
                plane = occy[0]
                for j in range(1, Y):
                    plane = plane + occy[j]
                occc[c] = plane
                stage_sends[2][0].start()
            if (t, k) == (0, 6):
                for d in ways:
                    lgot(d, 2).wait()
                    lshare(d, 2).start()
                ogot(2, occc, 1)
                occz[z] = occc[0] + occc[1]
                for copy in stage_sends[3]:
                    copy.start()
            if (t, k) == (1, 0):
                for d in ways:
                    for j in range(3):
                        lshared(d, j).wait()
                pltpu.make_async_copy(mine, mine, lsibr.at[6]).wait()
                for j in range(2):
                    keep_own(j).wait()
                multiply(0, 0, True)
                multiply(0, 1)
                multiply(0, -1)
            if (t, k) == (1, 1):
                multiply(0, 2)
                multiply(0, -2)
                multiply(0, 3)
            if (t, k) == (1, 2):
                multiply(0, -3)
                multiply(0, 4)
                turn(0)
                scatter(0, True)
            if (t, k) == (1, 3):
                multiply(1, 0, True)
                multiply(1, 1)
                multiply(1, -1)
            if (t, k) == (1, 4):
                multiply(1, 2)
                multiply(1, -2)
            if (t, k) == (1, 5):
                multiply(1, 3)
                multiply(1, -3)
            if (t, k) == (1, 6):
                multiply(1, 4)
                turn(1)
                scatter(1, True)

    ogot(3, occz, Z - 1)
    whole = occz[0]
    for j in range(1, Z):
        whole = whole + occz[j]
    mean = jnp.sum(whole, keepdims=True) / float(ROWS * 2 * Y)
    occ_ref[...] = jnp.broadcast_to(mean, (8, TILE))

    for d in ways:
        for t in range(2):
            for k in range(7):
                sent(d, t, k).wait_send()
        for k in range(3):
            lsent(d, k).wait_send()
            lshare(d, k).wait_send()
    for t in range(2):
        swap(t).wait_send()
    share_own.wait_send()
    for copies in stage_sends:
        for copy in copies:
            copy.wait_send()

    pltpu.make_async_copy(zin, zin, zrecv.at[0]).wait()
    square = zin[0]
    for j in range(1, Z):
        square = square + zin[j]
    square = jnp.concatenate([square, jnp.zeros((TILE - OUT, TILE), jnp.float32)], axis=0).T
    square = square[:ROWS, :OUT]
    doubled = 2.0 * win_ref[...].astype(jnp.float32) - square
    updated = jnp.where(branchm[:, :OUT] > 0.5, doubled, square)
    out_ref[...] = jnp.where(keepm[:, :OUT] > 0.5, updated, 0.0).astype(jnp.bfloat16)
    for t in range(2):
        scatter(t, False)


def shards(row_stripe, column_stripe, window_block, stripe_tiles, column_tiles, keep_tiles, branch):
    bf, f32 = jnp.bfloat16, jnp.float32
    dma = pltpu.SemaphoreType.DMA
    vmem = pl.BlockSpec(memory_space=pltpu.VMEM)
    block, occupancy = pl.pallas_call(
        kernel,
        out_shape=(
            jax.ShapeDtypeStruct((ROWS, OUT), bf),
            jax.ShapeDtypeStruct((8, TILE), f32),
        ),
        in_specs=[vmem] * 7,
        out_specs=(vmem, vmem),
        scratch_shapes=[
            pltpu.VMEM((4, SUB, TILE), bf),
            pltpu.VMEM((2, Y, KWIN, TILE), bf),
            pltpu.VMEM((X, 2 * ROWS_P, PANEL), bf),
            pltpu.VMEM((2, 2 * ROWS_P, TILE), f32),
            pltpu.VMEM((2, 2, TILE, TILE), f32),
            pltpu.VMEM((Z, OUT, TILE), f32),
            pltpu.VMEM((X, 8, TILE), f32),
            pltpu.VMEM((Y, 8, TILE), f32),
            pltpu.VMEM((2, 8, TILE), f32),
            pltpu.VMEM((Z, 8, TILE), f32),
            pltpu.VMEM((ROWS, TILE), f32),
            pltpu.VMEM((ROWS, TILE), f32),
            dma((28,)), dma((28,)),
            dma((2,)), dma((2,)), dma((2,)),
            dma((6,)), dma((6,)), dma((7,)), dma((7,)),
            dma((16,)), dma((1,)),
            dma((22,)), dma((4,)),
        ],
        compiler_params=pltpu.CompilerParams(
            collective_id=0, has_side_effects=True, vmem_limit_bytes=32 * 2**20
        ),
        name="square",
    )(row_stripe, column_stripe, window_block, stripe_tiles, column_tiles, keep_tiles, branch[None, :])
    return block, occupancy[0, 0]


def solution(mesh):
    return jax.shard_map(
        shards,
        mesh=mesh,
        in_specs=(
            P("row", "depth", "col"),
            P("depth", "row", "col"),
            P("row", ("col", "depth")),
            P(),
            P(),
            P(),
            P(),
        ),
        out_specs=(P("row", ("col", "depth")), P()),
        check_vma=False,
    )
```

time: 256 us -> 78.9 us (0.31)
  blocking collectives: 111 us -> 0 us
  waiting for transfers between devices: 111 us -> 0 us
  Pallas kernels: 0 us -> 73 us
  between operations: 15.9 us -> 0.71 us
  matrix products: 8.41 us -> 0 us
  other arithmetic: 4.66 us -> 0 us
    all_gather x2 -> x0, waiting for transfers between devices: 111 us -> none  [the longest x1 66.4 us: shards(): lax.all_gather(right_cols, 'row', axis=0, tiled=True)]
    psum x1 -> x0, blocking collectives: 111 us -> none  [shards(): occupancy = lax.psum(own_term, ('row', 'col', 'depth'))]
    pallas_call x0 -> x1, Pallas kernels: none -> 73 us  [shards(): pl.pallas_call(kernel, out_shape=(jax.ShapeDtypeStruct((ROWS, OUT), bf),...]
    dot_general x1 -> x0, matrix products: 8.41 us -> none  [shards(): jnp.dot(wide_left, lax.all_gather(right_cols, 'row', axis=0, tiled=True),...]
  transfers between devices with their start and end apart: 3 -> 0, of which waited for: 2 -> 0; matrix products, arithmetic and copies ran while one was open for 1% -> 0% of each run, Pallas kernels for 0% -> 0%
where the time goes in v1:
time: 78.9 us; the launch traced here: 78.7 us
  Pallas kernels  73 us (93%)
  local copies, waits for them, and re-layouts  4.94 us (6%)
    pallas_call x1, Pallas kernels, shards(): pl.pallas_call(kernel, out_shape=(jax.ShapeDtypeStruct((ROWS, OUT), bf),...  73 us
    unnamed x12, local copies, waits for them, and re-layouts  4.43 us

profile of v1, /device:TPU:1, one launch (start us, length us, event | category | flops | bytes accessed | tf_op | source)
XLA Modules:
  0.0 78.7 jit_solution(15317361771040306866)
XLA Ops:
  0.6 0.8 %copy.10.win_ref = bf16[120,40]{1,0:T(8,128)(2,1)S(1)} copy(bf16[120,40]{0,1:T(8,128)(2,1)} %param.9) | data formatting | bytes 19200 | tf_op args[2]
  1.4 1.0 %copy.11.ctab_ref = s32[816,15]{1,0:T(8,128)S(1)} copy(s32[816,15]{0,1:T(8,128)} %param.11) | data formatting | bytes 97920 | tf_op args[4]
  2.5 0.0 copy-start
  2.5 0.0 copy-start.1
  2.5 0.0 copy-start.2
  2.5 0.0 copy-start.3
  2.5 1.9 %copy.9.row_ref = bf16[120,1,2176]{2,1,0:T(2,128)(2,1)S(1)} copy(bf16[120,1,2176]{2,0,1:T(8,128)(2,1)} %param.7) | data formatting | bytes 1044480 | tf_op args[0]
  4.4 0.0 copy-done
  4.4 0.0 copy-done.1
  4.4 0.0 copy-done.2
  4.4 0.0 copy-done.3
  4.4 73.0 %square.1 = (bf16[120,40]{1,0:T(8,128)(2,1)S(1)}, f32[8,128]{1,0:T(8,128)S(1)}) custom-call(bf16[120,1,2176]{2,1,0:T(2,128)(2,1)S(1)} %copy.9.row_ref, bf16[1,544,480]{2,1,0:T(8,128)(2,1)S(1)} %copy-done, bf16[120,40]{1,0:T(8,128)(2,1)S(1)} %copy.10.win_ref, s32[15,816]{1,0:T(8,128)S(1)} %copy-done.1, s32[816,15]{1,0:T(8,128)S(1)} %copy.11.ctab_ref, ...), custom_call_target="tpu_custom_call" | custom-call | tf_op jit(solution)/shard_map/square/pallas_call | solution.py:413
  77.5 0.5 slice.3
  78.0 0.7 copy.12
Async XLA Ops:
  2.5 2.0 %copy-start = (bf16[1,544,480]{2,1,0:T(8,128)(2,1)S(1)}, bf16[1,544,480]{2,1,0:T(8,128)(2,1)}, u32[]{:S(2)}) copy-start(bf16[1,544,480]{2,1,0:T(8,128)(2,1)} %col_ref.1) | copy-start | bytes 1566724
  2.5 2.0 %copy-start.1 = (s32[15,816]{1,0:T(8,128)S(1)}, s32[15,816]{1,0:T(8,128)}, u32[]{:S(2)}) copy-start(s32[15,816]{1,0:T(8,128)} %stripe_ref.1) | copy-start | bytes 146884
  2.5 2.0 %copy-start.2 = (s32[15,15]{1,0:T(8,128)S(1)}, s32[15,15]{1,0:T(8,128)}, u32[]{:S(2)}) copy-start(s32[15,15]{1,0:T(8,128)} %keep_ref.1) | copy-start | bytes 2704
  2.5 1.9 %copy-start.3 = (s32[15]{0:T(128)S(1)}, s32[15]{0:T(128)}, u32[]{:S(2)}) copy-start(s32[15]{0:T(128)} %param.13) | copy-start | bytes 184

commit v2 on v1

--- a/solution.py
+++ b/solution.py
@@ -17,7 +17,9 @@
 COLS = 480
 OUT = 40
 KWIN = 1152
-EARLY = 1
+PART = 272
+EARLY = 4
+STEPS = 14
 
 
 def segments(tile):
@@ -38,11 +40,17 @@
     return jnp.dot(a, b, preferred_element_type=jnp.float32)
 
 
+def dot_t(a, b):
+    dims = (((1,), (1,)), ((), ()))
+    return lax.dot_general(a, b, dims, preferred_element_type=jnp.float32)
+
+
 def kernel(
-    row_ref, col_ref, win_ref, stripe_ref, ctab_ref, keep_ref, branch_ref,
+    row_in, col_in, win_in, stripe_in, ctab_in, keep_in, branch_in,
     out_ref, occ_ref,
+    row_ref, col_ref, win_ref, stripe_ref, ctab_ref, keep_ref, branch_ref, in_sem,
     rm, rb, lg, acc, ct, zin, occx, occy, occc, occz, keepm, branchm,
-    rsend, rrecv, dsend, drecv, own_sem, lsend, lrecv, lsibs, lsibr, zsend, zrecv, osend, orecv,
+    rsend, rrecv, go, dsend, drecv, own_sem, lsend, lrecv, lsibs, lsibr, zsend, zrecv, osend, orecv,
 ):
     r = lax.axis_index("row")
     x = lax.axis_index("col")
@@ -58,13 +66,36 @@
 
     sib = (y * 2 + (1 - c), x, z)
 
+    arrays = [
+        (ctab_in, ctab_ref), (col_in, col_ref), (stripe_in, stripe_ref), (row_in, row_ref),
+        (keep_in, keep_ref), (branch_in, branch_ref), (win_in, win_ref),
+    ]
+    loads = [pltpu.make_async_copy(a, b, in_sem.at[i]) for i, (a, b) in enumerate(arrays)]
+    for load in loads:
+        load.start()
+
     barrier = pltpu.get_barrier_semaphore()
-    peers = [ydev(d) for d in range(1, Y)] + [xdev(d) for d in range(1, X)] + [sib]
-    for d in range(1, Z):
-        peers.append((r, x, (z + d) % Z))
-        peers.append((y * 2 + (1 - c), x, (z + d) % Z))
-    for peer in peers:
+    plane = [((y + d) % Y * 2, x, z) for d in range(1, Y)] + [(y * 2, (x + d) % X, z) for d in range(1, X)]
+    others = [(y * 2 + 1, x, (z + d) % Z) for d in range(1, Z)]
+    for peer in plane:
         pl.semaphore_signal(barrier, inc=1, device_id=peer, device_id_type=MESH)
+
+    @pl.when(c == 1)
+    def _():
+        pl.semaphore_signal(barrier, inc=1, device_id=sib, device_id_type=MESH)
+
+    for peer in others:
+        pl.semaphore_signal(barrier, inc=1, device_id=peer, device_id_type=MESH)
+
+    def agree(counter, count, i):
+        @pl.when(c == counter)
+        def _():
+            pl.semaphore_wait(barrier, count)
+            pl.semaphore_signal(go.at[i], inc=1, device_id=sib, device_id_type=MESH)
+
+        @pl.when(c != counter)
+        def _():
+            pl.semaphore_wait(go.at[i], 1)
 
     for t in range(2):
         for yy in range(Y):
@@ -73,12 +104,13 @@
 
     first = z * 68 + (r * SUB) // TILE
     skew = (r * SUB) % TILE
+    loads[0].wait()
     ctab = one_hot(ctab_ref[...] > 0)
     pick = one_hot(
         lax.broadcasted_iota(jnp.int32, (16, 816), 1)
         == lax.broadcasted_iota(jnp.int32, (16, 816), 0) + first
     )
-    picked = dot(pick, ctab).astype(jnp.bfloat16)
+    picked = dot_t(pick, ctab).astype(jnp.bfloat16)
     spread = one_hot(
         lax.broadcasted_iota(jnp.int32, (15, 512), 0)
         == (lax.broadcasted_iota(jnp.int32, (15, 512), 1) + x * COLS) // TILE
@@ -88,62 +120,77 @@
         lax.broadcasted_iota(jnp.int32, (SUB, 16), 1)
         == (lax.broadcasted_iota(jnp.int32, (SUB, 16), 0) + skew) // TILE
     )
-    rm[3] = jnp.zeros((SUB, TILE), jnp.bfloat16)
-    for tile in range(4):
+
+    def masked(tile):
         wide = min(TILE, COLS - tile * TILE)
+        if wide < TILE:
+            rm[tile] = jnp.zeros((SUB, TILE), jnp.bfloat16)
         mask = dot(band, by_col[:, tile * TILE : tile * TILE + wide]).astype(jnp.bfloat16)
-        rm[tile, :, 0:wide] = col_ref[0, :, tile * TILE : tile * TILE + wide] * mask
-
-    pl.semaphore_wait(barrier, len(peers))
+        rm[tile, :, 0:wide] = col_ref[:, tile * TILE : tile * TILE + wide] * mask
+
+    loads[1].wait()
+    masked(0)
+    masked(1)
+
+    agree(0, 2 * len(plane) + 1, 0)
 
     def off(yy, cc):
         return pl.multiple_of((yy % 2) * 64 + cc * SUB, 32)
 
-    def piece(t, yy, cc):
-        return rb.at[t, yy, pl.ds(off(yy, cc), SUB), :]
+    def piece(t, yy, cc, part=None):
+        if part is None:
+            return rb.at[t, yy, pl.ds(off(yy, cc), SUB), :]
+        return rb.at[t, yy, pl.ds(pl.multiple_of(off(yy, cc) + part * PART, 16), PART), :]
 
     def which(d, k):
-        if k == 6:
-            return c if d > 0 else 1 - c
-        return c if k % 2 == 0 else 1 - c
+        if k >= 12:
+            return (c if d > 0 else 1 - c), k % 2
+        return (c if k % 4 < 2 else 1 - c), k % 2
 
     def sent(d, t, k):
-        yy = (y - d * (k // 2) + Y) % Y
-        there = piece(t, yy, which(d, k))
-        here = rm.at[2 * c + t] if k == 0 else there
-        i = (0 if d > 0 else 14) + t * 7 + k
+        yy = (y - d * (k // 4) + Y) % Y
+        core, part = which(d, k)
+        there = piece(t, yy, core, part)
+        here = rm.at[2 * t + c, part * PART : (part + 1) * PART, :] if k < 2 else there
+        i = ((0 if d > 0 else 2) + t) * STEPS + k
         return pltpu.make_async_remote_copy(
             src_ref=here, dst_ref=there, send_sem=rsend.at[i], recv_sem=rrecv.at[i],
             device_id=ydev(d % Y), device_id_type=MESH,
         )
 
     def got(d, t, k):
-        yy = (y - d * (k // 2 + 1) + Y) % Y
-        here = piece(t, yy, which(d, k))
-        i = (0 if d > 0 else 14) + t * 7 + k
+        yy = (y - d * (k // 4 + 1) + Y) % Y
+        here = piece(t, yy, *which(d, k))
+        i = ((0 if d > 0 else 2) + t) * STEPS + k
         return pltpu.make_async_copy(here, here, rrecv.at[i])
 
     ways = (1, -1)
-    for d in ways:
-        sent(d, 0, 0).start()
+    for k in range(2):
+        for d in ways:
+            sent(d, 0, k).start()
 
     def swap(t):
         return pltpu.make_async_remote_copy(
-            src_ref=rm.at[2 * (1 - c) + t], dst_ref=piece(t, y, c),
+            src_ref=rm.at[2 * t + 1 - c], dst_ref=piece(t, y, c),
             send_sem=dsend.at[t], recv_sem=drecv.at[t], device_id=sib, device_id_type=MESH,
         )
 
     def keep_own(t):
-        return pltpu.make_async_copy(rm.at[2 * c + t], piece(t, y, c), own_sem.at[t])
+        return pltpu.make_async_copy(rm.at[2 * t + c], piece(t, y, c), own_sem.at[t])
 
     def swapped(t):
         here = piece(t, y, 1 - c)
         return pltpu.make_async_copy(here, here, drecv.at[t])
 
-    for t in range(2):
-        swap(t).start()
-        keep_own(t).start()
-
+    swap(0).start()
+    keep_own(0).start()
+    masked(2)
+    masked(3)
+    swap(1).start()
+    keep_own(1).start()
+
+    loads[2].wait()
+    loads[3].wait()
     stab = one_hot(stripe_ref[...] > 0)
     base = z * 68 + x * 17
     shift = one_hot(
@@ -159,7 +206,7 @@
     total = jnp.zeros((8, TILE), jnp.float32)
     myrow = pl.multiple_of(c * ROWS_P, ROWS_P)
     for k in range(17):
-        part = row_ref[:, 0, k * TILE : k * TILE + TILE].astype(jnp.float32)
+        part = row_ref[:, k * TILE : k * TILE + TILE].astype(jnp.float32)
         part = part * lmask[:, k : k + 1]
         total = total + jnp.sum((part * part).reshape(15, 8, TILE), axis=0)
         whole = jnp.concatenate([part, jnp.zeros((8, TILE), jnp.float32)], axis=0)
@@ -218,8 +265,9 @@
     share_own.start()
 
     swapped(0).wait()
-    for d in ways:
-        sent(d, 0, 1).start()
+    for k in range(2, 4):
+        for d in ways:
+            sent(d, 0, k).start()
     swapped(1).wait()
     for k in range(EARLY):
         for d in ways:
@@ -245,16 +293,20 @@
     for copy in stage_sends[0]:
         copy.start()
 
+    for load in loads[4:]:
+        load.wait()
     tabk = one_hot(keep_ref[...] > 0)
     cols_in = one_hot(
-        lax.broadcasted_iota(jnp.int32, (15, TILE), 0)
-        == (lax.broadcasted_iota(jnp.int32, (15, TILE), 1) + x * COLS + z * OUT) // TILE
-    )
-    keepm[...] = dot(rows_in, dot(tabk, cols_in).astype(jnp.bfloat16))
-    flag = jnp.where(branch_ref[...] > 0, 1.0, 0.0)
-    branchm[...] = jnp.broadcast_to(
-        jnp.sum(rows_in.astype(jnp.float32) * flag, axis=1, keepdims=True), (ROWS, TILE)
-    )
+        lax.broadcasted_iota(jnp.int32, (OUT, 15), 1)
+        == (lax.broadcasted_iota(jnp.int32, (OUT, 15), 0) + x * COLS + z * OUT) // TILE
+    )
+    across = one_hot(
+        lax.broadcasted_iota(jnp.int32, (15, ROWS), 0)
+        == (lax.broadcasted_iota(jnp.int32, (15, ROWS), 1) + r * ROWS) // TILE
+    )
+    keepm[...] = dot(dot_t(cols_in, tabk).astype(jnp.bfloat16), across)
+    flag = jnp.broadcast_to(one_hot(branch_ref[...] > 0), (OUT, 15))
+    branchm[...] = dot(flag, across)
 
     def multiply(t, step, begin=False):
         yy = (y + step + Y) % Y
@@ -271,7 +323,7 @@
             @pl.when(c == n)
             def _():
                 i = t * 8
-                for zd, low, rows, at in segments(2 * n + t):
+                for zd, low, rows, at in segments(2 * t + n):
                     for cd in range(2):
                         src = ct.at[t, cd, pl.ds(low, rows), :]
                         dst = zin.at[z, pl.ds(at, rows), :]
@@ -299,46 +351,48 @@
             ct[t, cd] = acc[t, cd * TILE : cd * TILE + TILE, :].T
 
     for t in range(2):
-        for k in range(7):
+        for k in range(STEPS):
             for d in ways:
                 got(d, t, k).wait()
-                if k < 4:
-                    sent(d, t, k + 2).start()
-                if k == (4 if d > 0 else 5):
-                    sent(d, t, 6).start()
-                if t == 0 and k == 4:
-                    for j in range(EARLY, 2):
+                if k < 8:
+                    sent(d, t, k + 4).start()
+                if k in ((8, 9) if d > 0 else (10, 11)):
+                    sent(d, t, 12 + k % 2).start()
+                if t == 0 and k == 8:
+                    for j in range(EARLY, 4):
                         sent(d, 1, j).start()
-            if (t, k) == (0, 1):
+            if (t, k) == (0, 2):
                 for d in ways:
                     lgot(d, 0).wait()
                     lsent(d, 2).start()
                     lshare(d, 0).start()
-            if (t, k) == (0, 2):
+            if (t, k) == (0, 4):
                 ogot(0, occx, X - 1)
                 occy[y] = occx[0] + occx[1] + occx[2] + occx[3]
                 for copy in stage_sends[1]:
                     copy.start()
-            if (t, k) == (0, 4):
+            if (t, k) == (0, 6):
                 for d in ways:
                     lgot(d, 1).wait()
                     lshare(d, 1).start()
-            if (t, k) == (0, 5):
+            if (t, k) == (0, 8):
                 ogot(1, occy, Y - 1)
-                plane = occy[0]
+                summed = occy[0]
                 for j in range(1, Y):
-                    plane = plane + occy[j]
-                occc[c] = plane
+                    summed = summed + occy[j]
+                occc[c] = summed
                 stage_sends[2][0].start()
-            if (t, k) == (0, 6):
+            if (t, k) == (0, 10):
                 for d in ways:
                     lgot(d, 2).wait()
                     lshare(d, 2).start()
+            if (t, k) == (0, 11):
                 ogot(2, occc, 1)
                 occz[z] = occc[0] + occc[1]
+                agree(1, 2 * len(others), 1)
                 for copy in stage_sends[3]:
                     copy.start()
-            if (t, k) == (1, 0):
+            if (t, k) == (0, 12):
                 for d in ways:
                     for j in range(3):
                         lshared(d, j).wait()
@@ -348,26 +402,30 @@
                 multiply(0, 0, True)
                 multiply(0, 1)
                 multiply(0, -1)
-            if (t, k) == (1, 1):
+            if (t, k) == (0, 13):
                 multiply(0, 2)
                 multiply(0, -2)
+            if (t, k) == (1, 1):
                 multiply(0, 3)
-            if (t, k) == (1, 2):
                 multiply(0, -3)
+            if (t, k) == (1, 3):
                 multiply(0, 4)
                 turn(0)
                 scatter(0, True)
-            if (t, k) == (1, 3):
+            if (t, k) == (1, 5):
                 multiply(1, 0, True)
+            if (t, k) == (1, 6):
                 multiply(1, 1)
+            if (t, k) == (1, 7):
                 multiply(1, -1)
-            if (t, k) == (1, 4):
+            if (t, k) == (1, 8):
                 multiply(1, 2)
+            if (t, k) == (1, 9):
                 multiply(1, -2)
-            if (t, k) == (1, 5):
+            if (t, k) == (1, 11):
                 multiply(1, 3)
                 multiply(1, -3)
-            if (t, k) == (1, 6):
+            if (t, k) == (1, 13):
                 multiply(1, 4)
                 turn(1)
                 scatter(1, True)
@@ -377,11 +435,11 @@
     for j in range(1, Z):
         whole = whole + occz[j]
     mean = jnp.sum(whole, keepdims=True) / float(ROWS * 2 * Y)
-    occ_ref[...] = jnp.broadcast_to(mean, (8, TILE))
+    occ_ref[...] = mean
 
     for d in ways:
         for t in range(2):
-            for k in range(7):
+            for k in range(STEPS):
                 sent(d, t, k).wait_send()
         for k in range(3):
             lsent(d, k).wait_send()
@@ -397,11 +455,10 @@
     square = zin[0]
     for j in range(1, Z):
         square = square + zin[j]
-    square = jnp.concatenate([square, jnp.zeros((TILE - OUT, TILE), jnp.float32)], axis=0).T
-    square = square[:ROWS, :OUT]
+    square = square[:, :ROWS]
     doubled = 2.0 * win_ref[...].astype(jnp.float32) - square
-    updated = jnp.where(branchm[:, :OUT] > 0.5, doubled, square)
-    out_ref[...] = jnp.where(keepm[:, :OUT] > 0.5, updated, 0.0).astype(jnp.bfloat16)
+    updated = jnp.where(branchm[...] > 0.5, doubled, square)
+    out_ref[...] = jnp.where(keepm[...] > 0.5, updated, 0.0).astype(jnp.bfloat16)
     for t in range(2):
         scatter(t, False)
 
@@ -413,12 +470,20 @@
     block, occupancy = pl.pallas_call(
         kernel,
         out_shape=(
-            jax.ShapeDtypeStruct((ROWS, OUT), bf),
-            jax.ShapeDtypeStruct((8, TILE), f32),
+            jax.ShapeDtypeStruct((OUT, ROWS), bf),
+            jax.ShapeDtypeStruct((1, 1), f32),
         ),
-        in_specs=[vmem] * 7,
+        in_specs=[pl.BlockSpec(memory_space=pl.ANY)] * 7,
         out_specs=(vmem, vmem),
         scratch_shapes=[
+            pltpu.VMEM((ROWS, PANEL), bf),
+            pltpu.VMEM((SUB, COLS), bf),
+            pltpu.VMEM((OUT, ROWS), bf),
+            pltpu.VMEM((15, 816), jnp.int32),
+            pltpu.VMEM((15, 816), jnp.int32),
+            pltpu.VMEM((15, 15), jnp.int32),
+            pltpu.VMEM((1, 15), jnp.int32),
+            dma((7,)),
             pltpu.VMEM((4, SUB, TILE), bf),
             pltpu.VMEM((2, Y, KWIN, TILE), bf),
             pltpu.VMEM((X, 2 * ROWS_P, PANEL), bf),
@@ -429,20 +494,23 @@
             pltpu.VMEM((Y, 8, TILE), f32),
             pltpu.VMEM((2, 8, TILE), f32),
             pltpu.VMEM((Z, 8, TILE), f32),
-            pltpu.VMEM((ROWS, TILE), f32),
-            pltpu.VMEM((ROWS, TILE), f32),
-            dma((28,)), dma((28,)),
+            pltpu.VMEM((OUT, ROWS), f32),
+            pltpu.VMEM((OUT, ROWS), f32),
+            dma((4 * STEPS,)), dma((4 * STEPS,)), pltpu.SemaphoreType.REGULAR((2,)),
             dma((2,)), dma((2,)), dma((2,)),
             dma((6,)), dma((6,)), dma((7,)), dma((7,)),
             dma((16,)), dma((1,)),
             dma((22,)), dma((4,)),
         ],
         compiler_params=pltpu.CompilerParams(
-            collective_id=0, has_side_effects=True, vmem_limit_bytes=32 * 2**20
+            collective_id=0, has_side_effects=True, vmem_limit_bytes=56 * 2**20
         ),
         name="square",
-    )(row_stripe, column_stripe, window_block, stripe_tiles, column_tiles, keep_tiles, branch[None, :])
-    return block, occupancy[0, 0]
+    )(
+        row_stripe[:, 0, :], column_stripe[0], window_block.T, stripe_tiles, column_tiles.T,
+        keep_tiles, branch[None, :],
+    )
+    return block.T, occupancy[0, 0]
 
 
 def solution(mesh):

time: 78.9 us -> 70.8 us (0.90)
  Pallas kernels: 73 us -> 66.2 us
  local copies, waits for them, and re-layouts: 4.94 us -> 1.3 us
  between operations: 0.71 us -> 2.4 us
    pallas_call x1, Pallas kernels: 73 us -> 66.2 us  [shards(): pl.pallas_call(kernel, out_shape=(jax.ShapeDtypeStruct((OUT, ROWS), bf),...]
    unnamed x12 -> x1, local copies, waits for them, and re-layouts: 4.43 us -> 1.3 us
where the time goes in v2:
time: 70.8 us; the launch traced here: 69.9 us
  Pallas kernels  66.2 us (94%)
  between operations  2.4 us (3%)
  local copies, waits for them, and re-layouts  1.3 us (2%)
    pallas_call x1, Pallas kernels, shards(): pl.pallas_call(kernel, out_shape=(jax.ShapeDtypeStruct((OUT, ROWS), bf),...  66.2 us

profile of v2, /device:TPU:1, one launch (start us, length us, event | category | flops | bytes accessed | tf_op | source)
XLA Modules:
  0.0 69.9 jit_solution(8718117382909113083)
XLA Ops:
  0.6 66.2 %square.1 = (bf16[40,120]{1,0:T(8,128)(2,1)}, f32[1,1]{1,0:T(1,128)}) custom-call(bf16[120,2176]{1,0:T(8,128)(2,1)} %bitcast.8, bf16[544,480]{1,0:T(8,128)(2,1)} %bitcast.7, bf16[40,120]{1,0:T(8,128)(2,1)} %bitcast.10, s32[15,816]{1,0:T(8,128)} %stripe_in.1, s32[15,816]{1,0:T(8,128)} %bitcast.9, s32[15,15]{1,0:T(8,128)} %keep_in.1, s32[1,15]{1,0:T(1,128)} %bitcast.12), custom_call_target="tpu_custom_call" | custom-call | tf_op jit(solution)/shard_map/square/pallas_call | solution.py:470
  66.8 1.3 %copy.11 = bf16[120,40]{0,1:T(8,128)(2,1)} copy(bf16[120,40]{0,1:T(8,128)(2,1)} %bitcast.11) | data formatting | bytes 19200

commit v3 on v2

--- a/solution.py
+++ b/solution.py
@@ -18,7 +18,7 @@
 OUT = 40
 KWIN = 1152
 PART = 272
-EARLY = 4
+EARLY = 3
 STEPS = 14
 
 
@@ -84,9 +84,6 @@
     def _():
         pl.semaphore_signal(barrier, inc=1, device_id=sib, device_id_type=MESH)
 
-    for peer in others:
-        pl.semaphore_signal(barrier, inc=1, device_id=peer, device_id_type=MESH)
-
     def agree(counter, count, i):
         @pl.when(c == counter)
         def _():
@@ -129,8 +126,11 @@
         rm[tile, :, 0:wide] = col_ref[:, tile * TILE : tile * TILE + wide] * mask
 
     loads[1].wait()
-    masked(0)
-    masked(1)
+    for n in range(2):
+
+        @pl.when(c == n)
+        def _():
+            masked(n)
 
     agree(0, 2 * len(plane) + 1, 0)
 
@@ -143,8 +143,8 @@
         return rb.at[t, yy, pl.ds(pl.multiple_of(off(yy, cc) + part * PART, 16), PART), :]
 
     def which(d, k):
-        if k >= 12:
-            return (c if d > 0 else 1 - c), k % 2
+        if k >= 8 and d < 0:
+            return (1 - c if k % 4 < 2 else c), k % 2
         return (c if k % 4 < 2 else 1 - c), k % 2
 
     def sent(d, t, k):
@@ -158,6 +158,11 @@
             device_id=ydev(d % Y), device_id_type=MESH,
         )
 
+    def passed(d, k):
+        if 4 <= k < 8 and d < 0:
+            return 8 + (k - 4 + 2) % 4
+        return k + 4
+
     def got(d, t, k):
         yy = (y - d * (k // 4 + 1) + Y) % Y
         here = piece(t, yy, *which(d, k))
@@ -182,8 +187,16 @@
         here = piece(t, y, 1 - c)
         return pltpu.make_async_copy(here, here, drecv.at[t])
 
+    for n in range(2):
+
+        @pl.when(c != n)
+        def _():
+            masked(n)
+
     swap(0).start()
     keep_own(0).start()
+    for peer in others:
+        pl.semaphore_signal(barrier, inc=1, device_id=peer, device_id_type=MESH)
     masked(2)
     masked(3)
     swap(1).start()
@@ -350,85 +363,81 @@
         for cd in range(2):
             ct[t, cd] = acc[t, cd * TILE : cd * TILE + TILE, :].T
 
-    for t in range(2):
-        for k in range(STEPS):
+    order = [(0, k) for k in range(10)] + [(1, 0), (1, 1), (0, 10), (0, 11), (1, 2), (1, 3)]
+    order += [(0, 12), (0, 13)] + [(1, k) for k in range(4, STEPS)]
+    for t, k in order:
+        for d in ways:
+            got(d, t, k).wait()
+            if k < 10:
+                sent(d, t, passed(d, k)).start()
+            if (t, k) == (0, 7):
+                for j in range(EARLY, 4):
+                    sent(d, 1, j).start()
+        if (t, k) == (0, 2):
             for d in ways:
-                got(d, t, k).wait()
-                if k < 8:
-                    sent(d, t, k + 4).start()
-                if k in ((8, 9) if d > 0 else (10, 11)):
-                    sent(d, t, 12 + k % 2).start()
-                if t == 0 and k == 8:
-                    for j in range(EARLY, 4):
-                        sent(d, 1, j).start()
-            if (t, k) == (0, 2):
-                for d in ways:
-                    lgot(d, 0).wait()
-                    lsent(d, 2).start()
-                    lshare(d, 0).start()
-            if (t, k) == (0, 4):
-                ogot(0, occx, X - 1)
-                occy[y] = occx[0] + occx[1] + occx[2] + occx[3]
-                for copy in stage_sends[1]:
-                    copy.start()
-            if (t, k) == (0, 6):
-                for d in ways:
-                    lgot(d, 1).wait()
-                    lshare(d, 1).start()
-            if (t, k) == (0, 8):
-                ogot(1, occy, Y - 1)
-                summed = occy[0]
-                for j in range(1, Y):
-                    summed = summed + occy[j]
-                occc[c] = summed
-                stage_sends[2][0].start()
-            if (t, k) == (0, 10):
-                for d in ways:
-                    lgot(d, 2).wait()
-                    lshare(d, 2).start()
-            if (t, k) == (0, 11):
-                ogot(2, occc, 1)
-                occz[z] = occc[0] + occc[1]
-                agree(1, 2 * len(others), 1)
-                for copy in stage_sends[3]:
-                    copy.start()
-            if (t, k) == (0, 12):
-                for d in ways:
-                    for j in range(3):
-                        lshared(d, j).wait()
-                pltpu.make_async_copy(mine, mine, lsibr.at[6]).wait()
-                for j in range(2):
-                    keep_own(j).wait()
-                multiply(0, 0, True)
-                multiply(0, 1)
-                multiply(0, -1)
-            if (t, k) == (0, 13):
-                multiply(0, 2)
-                multiply(0, -2)
-            if (t, k) == (1, 1):
-                multiply(0, 3)
-                multiply(0, -3)
-            if (t, k) == (1, 3):
-                multiply(0, 4)
-                turn(0)
-                scatter(0, True)
-            if (t, k) == (1, 5):
-                multiply(1, 0, True)
-            if (t, k) == (1, 6):
-                multiply(1, 1)
-            if (t, k) == (1, 7):
-                multiply(1, -1)
-            if (t, k) == (1, 8):
-                multiply(1, 2)
-            if (t, k) == (1, 9):
-                multiply(1, -2)
-            if (t, k) == (1, 11):
-                multiply(1, 3)
-                multiply(1, -3)
-            if (t, k) == (1, 13):
-                multiply(1, 4)
-                turn(1)
-                scatter(1, True)
+                lgot(d, 0).wait()
+                lsent(d, 2).start()
+                lshare(d, 0).start()
+        if (t, k) == (0, 5):
+            ogot(0, occx, X - 1)
+            occy[y] = occx[0] + occx[1] + occx[2] + occx[3]
+            for copy in stage_sends[1]:
+                copy.start()
+        if (t, k) == (0, 7):
+            for d in ways:
+                lgot(d, 1).wait()
+                lshare(d, 1).start()
+        if (t, k) == (0, 9):
+            ogot(1, occy, Y - 1)
+            summed = occy[0]
+            for j in range(1, Y):
+                summed = summed + occy[j]
+            occc[c] = summed
+            stage_sends[2][0].start()
+        if (t, k) == (1, 3):
+            for d in ways:
+                lgot(d, 2).wait()
+                lshare(d, 2).start()
+        if (t, k) == (0, 12):
+            for d in ways:
+                for j in range(3):
+                    lshared(d, j).wait()
+            pltpu.make_async_copy(mine, mine, lsibr.at[6]).wait()
+            for j in range(2):
+                keep_own(j).wait()
+            multiply(0, 0, True)
+            multiply(0, 1)
+            multiply(0, -1)
+            ogot(2, occc, 1)
+            occz[z] = occc[0] + occc[1]
+            agree(1, 2 * len(others), 1)
+            for copy in stage_sends[3]:
+                copy.start()
+        if (t, k) == (0, 13):
+            multiply(0, 2)
+            multiply(0, -2)
+        if (t, k) == (1, 4):
+            multiply(0, 3)
+            multiply(0, -3)
+        if (t, k) == (1, 5):
+            multiply(0, 4)
+            turn(0)
+            scatter(0, True)
+        if (t, k) == (1, 8):
+            multiply(1, 0, True)
+            multiply(1, 1)
+        if (t, k) == (1, 9):
+            multiply(1, -1)
+            multiply(1, 2)
+        if (t, k) == (1, 10):
+            multiply(1, -2)
+        if (t, k) == (1, 11):
+            multiply(1, 3)
+            multiply(1, -3)
+        if (t, k) == (1, 13):
+            multiply(1, 4)
+            turn(1)
+            scatter(1, True)
 
     ogot(3, occz, Z - 1)
     whole = occz[0]

time: 70.8 us -> 68.9 us (0.973); the launches traced: 69.9 us -> 68.7 us
  Pallas kernels: 66.2 us -> 65 us
    pallas_call x1, Pallas kernels: 66.2 us -> 65 us  [shards(): pl.pallas_call(kernel, out_shape=(jax.ShapeDtypeStruct((OUT, ROWS), bf),...]
where the time goes in v3:
time: 68.9 us; the launch traced here: 68.7 us
  Pallas kernels  65 us (94%)
  between operations  2.4 us (3%)
  local copies, waits for them, and re-layouts  1.3 us (2%)
    pallas_call x1, Pallas kernels, shards(): pl.pallas_call(kernel, out_shape=(jax.ShapeDtypeStruct((OUT, ROWS), bf),...  65 us

profile of v3, /device:TPU:1, one launch (start us, length us, event | category | flops | bytes accessed | tf_op | source)
XLA Modules:
  0.0 68.7 jit_solution(683092818601015100)
XLA Ops:
  0.6 65.0 %square.1 = (bf16[40,120]{1,0:T(8,128)(2,1)}, f32[1,1]{1,0:T(1,128)}) custom-call(bf16[120,2176]{1,0:T(8,128)(2,1)} %bitcast.8, bf16[544,480]{1,0:T(8,128)(2,1)} %bitcast.7, bf16[40,120]{1,0:T(8,128)(2,1)} %bitcast.10, s32[15,816]{1,0:T(8,128)} %stripe_in.1, s32[15,816]{1,0:T(8,128)} %bitcast.9, s32[15,15]{1,0:T(8,128)} %keep_in.1, s32[1,15]{1,0:T(1,128)} %bitcast.12), custom_call_target="tpu_custom_call" | custom-call | tf_op jit(solution)/shard_map/square/pallas_call | solution.py:479
  65.7 1.3 %copy.11 = bf16[120,40]{0,1:T(8,128)(2,1)} copy(bf16[120,40]{0,1:T(8,128)(2,1)} %bitcast.11) | data formatting | bytes 19200

commit v4 on v2

--- a/solution.py
+++ b/solution.py
@@ -18,8 +18,10 @@
 OUT = 40
 KWIN = 1152
 PART = 272
-EARLY = 4
+EARLY = 3
 STEPS = 14
+LAST = COLS - 3 * TILE
+SPARE = TILE - LAST
 
 
 def segments(tile):
@@ -32,6 +34,20 @@
     return found
 
 
+def hops(d, t, core):
+    if t == 1 and core == 1:
+        first = [2 * PART, 0, PART]
+        third = first if d > 0 else [PART, 2 * PART, 0]
+        fourth = first[:2] if d > 0 else [PART]
+    else:
+        own = [core * SUB, core * SUB + PART]
+        other = [SUB - core * SUB, SUB - core * SUB + PART]
+        first = own + other
+        third = first if d > 0 else other + own
+        fourth = own if d > 0 else other
+    return [(h + 1, row) for h, rows in enumerate((first, first, third, fourth)) for row in rows]
+
+
 def one_hot(hit):
     return jnp.where(hit, 1.0, 0.0).astype(jnp.bfloat16)
 
@@ -49,7 +65,7 @@
     row_in, col_in, win_in, stripe_in, ctab_in, keep_in, branch_in,
     out_ref, occ_ref,
     row_ref, col_ref, win_ref, stripe_ref, ctab_ref, keep_ref, branch_ref, in_sem,
-    rm, rb, lg, acc, ct, zin, occx, occy, occc, occz, keepm, branchm,
+    rm, rb, lg, acc, ct, zin, occx, occy, occc, occz, keepm, branchm, um,
     rsend, rrecv, go, dsend, drecv, own_sem, lsend, lrecv, lsibs, lsibr, zsend, zrecv, osend, orecv,
 ):
     r = lax.axis_index("row")
@@ -84,9 +100,6 @@
     def _():
         pl.semaphore_signal(barrier, inc=1, device_id=sib, device_id_type=MESH)
 
-    for peer in others:
-        pl.semaphore_signal(barrier, inc=1, device_id=peer, device_id_type=MESH)
-
     def agree(counter, count, i):
         @pl.when(c == counter)
         def _():
@@ -129,45 +142,47 @@
         rm[tile, :, 0:wide] = col_ref[:, tile * TILE : tile * TILE + wide] * mask
 
     loads[1].wait()
-    masked(0)
-    masked(1)
+    for n in range(2):
+
+        @pl.when(c == n)
+        def _():
+            masked(n)
 
     agree(0, 2 * len(plane) + 1, 0)
 
     def off(yy, cc):
         return pl.multiple_of((yy % 2) * 64 + cc * SUB, 32)
 
-    def piece(t, yy, cc, part=None):
-        if part is None:
-            return rb.at[t, yy, pl.ds(off(yy, cc), SUB), :]
-        return rb.at[t, yy, pl.ds(pl.multiple_of(off(yy, cc) + part * PART, 16), PART), :]
-
-    def which(d, k):
-        if k >= 12:
-            return (c if d > 0 else 1 - c), k % 2
-        return (c if k % 4 < 2 else 1 - c), k % 2
-
-    def sent(d, t, k):
-        yy = (y - d * (k // 4) + Y) % Y
-        core, part = which(d, k)
-        there = piece(t, yy, core, part)
-        here = rm.at[2 * t + c, part * PART : (part + 1) * PART, :] if k < 2 else there
+    def piece(t, yy, cc):
+        return rb.at[t, yy, pl.ds(off(yy, cc), SUB), :]
+
+    def block(t, yy, row):
+        start = pl.multiple_of((yy % 2) * 64 + row, 16)
+        return rb.at[t, yy, pl.ds(start, PART), :]
+
+    def sent(d, t, k, row, hop, here=None):
+        there = block(t, (y - d * (hop - 1) + Y) % Y, row)
         i = ((0 if d > 0 else 2) + t) * STEPS + k
         return pltpu.make_async_remote_copy(
-            src_ref=here, dst_ref=there, send_sem=rsend.at[i], recv_sem=rrecv.at[i],
-            device_id=ydev(d % Y), device_id_type=MESH,
+            src_ref=there if here is None else here, dst_ref=there, send_sem=rsend.at[i],
+            recv_sem=rrecv.at[i], device_id=ydev(d % Y), device_id_type=MESH,
         )
 
-    def got(d, t, k):
-        yy = (y - d * (k // 4 + 1) + Y) % Y
-        here = piece(t, yy, *which(d, k))
+    def got(d, t, k, row, hop):
+        here = block(t, (y - d * hop + Y) % Y, row)
         i = ((0 if d > 0 else 2) + t) * STEPS + k
         return pltpu.make_async_copy(here, here, rrecv.at[i])
+
+    def first_hop(d, t, k):
+        part = (k % 2) * PART
+        if k < 2:
+            return sent(d, t, k, c * SUB + part, 1, rm.at[2 * t + c, part : part + PART, :])
+        return sent(d, t, k, (1 - c) * SUB + part, 1)
 
     ways = (1, -1)
     for k in range(2):
         for d in ways:
-            sent(d, 0, k).start()
+            first_hop(d, 0, k).start()
 
     def swap(t):
         return pltpu.make_async_remote_copy(
@@ -182,12 +197,24 @@
         here = piece(t, y, 1 - c)
         return pltpu.make_async_copy(here, here, drecv.at[t])
 
+    for n in range(2):
+
+        @pl.when(c != n)
+        def _():
+            masked(n)
+
     swap(0).start()
     keep_own(0).start()
+    for peer in others:
+        pl.semaphore_signal(barrier, inc=1, device_id=peer, device_id_type=MESH)
     masked(2)
     masked(3)
     swap(1).start()
-    keep_own(1).start()
+
+    @pl.when(c == 0)
+    def _():
+        keep_own(1).start()
+
 
     loads[2].wait()
     loads[3].wait()
@@ -267,11 +294,32 @@
     swapped(0).wait()
     for k in range(2, 4):
         for d in ways:
-            sent(d, 0, k).start()
+            first_hop(d, 0, k).start()
+
+    lane_in = lax.broadcasted_iota(jnp.int32, (TILE, TILE), 0)
+    lane_out = lax.broadcasted_iota(jnp.int32, (TILE, TILE), 1)
+    for g in range(3):
+        um[g] = one_hot((lane_in >= LAST) & (lane_in - LAST + g * SPARE == lane_out))
+
     swapped(1).wait()
-    for k in range(EARLY):
-        for d in ways:
-            sent(d, 1, k).start()
+
+    @pl.when(c == 0)
+    def _():
+        for k in range(EARLY):
+            for d in ways:
+                first_hop(d, 1, k).start()
+
+    @pl.when(c == 1)
+    def _():
+        fourth = rm[3, PART:SUB, :]
+        block(1, y, 3 * PART)[...] = fourth
+        for g in (2, 0, 1):
+            main = rm[3, 0:PART, :] if g == 2 else block(1, y, g * PART)[...]
+            extra = dot_t(fourth, um[g])
+            block(1, y, g * PART)[...] = (main.astype(jnp.float32) + extra).astype(jnp.bfloat16)
+        for k in range(min(EARLY, 3)):
+            for d in ways:
+                sent(d, 1, k, *hops(d, 1, 1)[k][::-1]).start()
 
     def osent(stage, i, buf, slot, device):
         return pltpu.make_async_remote_copy(
@@ -308,8 +356,13 @@
     flag = jnp.broadcast_to(one_hot(branch_ref[...] > 0), (OUT, 15))
     branchm[...] = dot(flag, across)
 
-    def multiply(t, step, begin=False):
+    def multiply(n, t, step, begin=False):
         yy = (y + step + Y) % Y
+        if t == 1 and n == 1 and step != 0:
+            fourth = dot(block(1, yy, 0)[...], um[0])
+            for g in (1, 2):
+                fourth = fourth + dot(block(1, yy, g * PART)[...], um[g])
+            block(1, yy, 3 * PART)[...] = fourth.astype(jnp.bfloat16)
         window = pl.multiple_of((yy % 2) * 1024, 1024)
         product = dot(lg[yy // 2, :, pl.ds(window, KWIN)], rb[t, yy])
         if begin:
@@ -350,85 +403,111 @@
         for cd in range(2):
             ct[t, cd] = acc[t, cd * TILE : cd * TILE + TILE, :].T
 
-    for t in range(2):
-        for k in range(STEPS):
+    points = (
+        dict(
+            la=(0, 2), o1=(0, 5), lb=(0, 7), o2=(0, 9), lf=(1, 3), m0a=(0, 12), m0b=(0, 13), m0c=(1, 4),
+            m0d=(1, 5), m1a=(1, 8), m1b=(1, 9), m1c=(1, 10), m1d=(1, 11), end=(1, 13),
+        ),
+        dict(
+            la=(0, 2), o1=(0, 5), lb=(0, 7), o2=(0, 9), lf=(1, 2), m0a=(0, 12), m0b=(0, 13), m0c=(1, 3),
+            m0d=(1, 4), m1a=(1, 6), m1b=(1, 7), m1c=(1, 8), m1d=(1, 9), end=(1, 10),
+        ),
+    )
+
+    def ring(n):
+        at = points[n]
+        pieces = {(d, t): hops(d, t, n) for d in ways for t in range(2)}
+        order = [(0, k) for k in range(10)] + [(1, 0), (1, 1), (0, 10), (0, 11)]
+        order += ([(1, 2), (1, 3)] if n == 0 else [(1, 2)]) + [(0, 12), (0, 13)]
+        order += [(1, k) for k in (range(4, 14) if n == 0 else range(3, 11))]
+        for t, k in order:
             for d in ways:
-                got(d, t, k).wait()
-                if k < 8:
-                    sent(d, t, k + 4).start()
-                if k in ((8, 9) if d > 0 else (10, 11)):
-                    sent(d, t, 12 + k % 2).start()
-                if t == 0 and k == 8:
-                    for j in range(EARLY, 4):
-                        sent(d, 1, j).start()
-            if (t, k) == (0, 2):
+                mine_d = pieces[d, t]
+                if k < len(mine_d):
+                    hop, row = mine_d[k]
+                    got(d, t, k, row, hop).wait()
+                    if (hop + 1, row) in mine_d:
+                        sent(d, t, mine_d.index((hop + 1, row)), row, hop + 1).start()
+                if (t, k) == (0, 7):
+                    for j in range(EARLY, 4 - n):
+                        if n == 0:
+                            first_hop(d, 1, j).start()
+                        else:
+                            sent(d, 1, j, *pieces[d, 1][j][::-1]).start()
+            if (t, k) == at["la"]:
                 for d in ways:
                     lgot(d, 0).wait()
                     lsent(d, 2).start()
                     lshare(d, 0).start()
-            if (t, k) == (0, 4):
+            if (t, k) == at["o1"]:
                 ogot(0, occx, X - 1)
                 occy[y] = occx[0] + occx[1] + occx[2] + occx[3]
                 for copy in stage_sends[1]:
                     copy.start()
-            if (t, k) == (0, 6):
+            if (t, k) == at["lb"]:
                 for d in ways:
                     lgot(d, 1).wait()
                     lshare(d, 1).start()
-            if (t, k) == (0, 8):
+            if (t, k) == at["o2"]:
                 ogot(1, occy, Y - 1)
                 summed = occy[0]
                 for j in range(1, Y):
                     summed = summed + occy[j]
                 occc[c] = summed
                 stage_sends[2][0].start()
-            if (t, k) == (0, 10):
+            if (t, k) == at["lf"]:
                 for d in ways:
                     lgot(d, 2).wait()
                     lshare(d, 2).start()
-            if (t, k) == (0, 11):
+            if (t, k) == at["m0a"]:
+                for d in ways:
+                    for j in range(3):
+                        lshared(d, j).wait()
+                pltpu.make_async_copy(mine, mine, lsibr.at[6]).wait()
+                for j in range(2 - n):
+                    keep_own(j).wait()
+                multiply(n, 0, 0, True)
+                multiply(n, 0, 1)
+                multiply(n, 0, -1)
                 ogot(2, occc, 1)
                 occz[z] = occc[0] + occc[1]
                 agree(1, 2 * len(others), 1)
                 for copy in stage_sends[3]:
                     copy.start()
-            if (t, k) == (0, 12):
-                for d in ways:
-                    for j in range(3):
-                        lshared(d, j).wait()
-                pltpu.make_async_copy(mine, mine, lsibr.at[6]).wait()
-                for j in range(2):
-                    keep_own(j).wait()
-                multiply(0, 0, True)
-                multiply(0, 1)
-                multiply(0, -1)
-            if (t, k) == (0, 13):
-                multiply(0, 2)
-                multiply(0, -2)
-            if (t, k) == (1, 1):
-                multiply(0, 3)
-                multiply(0, -3)
-            if (t, k) == (1, 3):
-                multiply(0, 4)
+            if (t, k) == at["m0b"]:
+                multiply(n, 0, 2)
+                multiply(n, 0, -2)
+            if (t, k) == at["m0c"]:
+                multiply(n, 0, 3)
+                multiply(n, 0, -3)
+            if (t, k) == at["m0d"]:
+                multiply(n, 0, 4)
                 turn(0)
                 scatter(0, True)
-            if (t, k) == (1, 5):
-                multiply(1, 0, True)
-            if (t, k) == (1, 6):
-                multiply(1, 1)
-            if (t, k) == (1, 7):
-                multiply(1, -1)
-            if (t, k) == (1, 8):
-                multiply(1, 2)
-            if (t, k) == (1, 9):
-                multiply(1, -2)
-            if (t, k) == (1, 11):
-                multiply(1, 3)
-                multiply(1, -3)
-            if (t, k) == (1, 13):
-                multiply(1, 4)
+            if (t, k) == at["m1a"]:
+                multiply(n, 1, 0, True)
+                multiply(n, 1, 1)
+            if (t, k) == at["m1b"]:
+                multiply(n, 1, -1)
+                multiply(n, 1, 2)
+            if (t, k) == at["m1c"]:
+                multiply(n, 1, -2)
+            if (t, k) == at["m1d"]:
+                multiply(n, 1, 3)
+                multiply(n, 1, -3)
+            if (t, k) == at["end"]:
+                multiply(n, 1, 4)
                 turn(1)
                 scatter(1, True)
+        for (d, t), listed in pieces.items():
+            for k, (hop, row) in enumerate(listed):
+                sent(d, t, k, row, hop).wait_send()
+
+    for n in range(2):
+
+        @pl.when(c == n)
+        def _():
+            ring(n)
 
     ogot(3, occz, Z - 1)
     whole = occz[0]
@@ -438,9 +517,6 @@
     occ_ref[...] = mean
 
     for d in ways:
-        for t in range(2):
-            for k in range(STEPS):
-                sent(d, t, k).wait_send()
         for k in range(3):
             lsent(d, k).wait_send()
             lshare(d, k).wait_send()
@@ -496,6 +572,7 @@
             pltpu.VMEM((Z, 8, TILE), f32),
             pltpu.VMEM((OUT, ROWS), f32),
             pltpu.VMEM((OUT, ROWS), f32),
+            pltpu.VMEM((3, TILE, TILE), bf),
             dma((4 * STEPS,)), dma((4 * STEPS,)), pltpu.SemaphoreType.REGULAR((2,)),
             dma((2,)), dma((2,)), dma((2,)),
             dma((6,)), dma((6,)), dma((7,)), dma((7,)),

time: 70.8 us -> 66.9 us (0.945)
  Pallas kernels: 66.2 us -> 63 us
    pallas_call x1, Pallas kernels: 66.2 us -> 63 us  [shards(): pl.pallas_call(kernel, out_shape=(jax.ShapeDtypeStruct((OUT, ROWS), bf),...]
where the time goes in v4:
time: 66.9 us; the launch traced here: 66.7 us
  Pallas kernels  63 us (94%)
  between operations  2.4 us (4%)
  local copies, waits for them, and re-layouts  1.3 us (2%)
    pallas_call x1, Pallas kernels, shards(): pl.pallas_call(kernel, out_shape=(jax.ShapeDtypeStruct((OUT, ROWS), bf),...  63 us

profile of v4, /device:TPU:1, one launch (start us, length us, event | category | flops | bytes accessed | tf_op | source)
XLA Modules:
  0.0 66.7 jit_solution(15589083200053658724)
XLA Ops:
  0.6 63.0 %square.1 = (bf16[40,120]{1,0:T(8,128)(2,1)}, f32[1,1]{1,0:T(1,128)}) custom-call(bf16[120,2176]{1,0:T(8,128)(2,1)} %bitcast.8, bf16[544,480]{1,0:T(8,128)(2,1)} %bitcast.7, bf16[40,120]{1,0:T(8,128)(2,1)} %bitcast.10, s32[15,816]{1,0:T(8,128)} %stripe_in.1, s32[15,816]{1,0:T(8,128)} %bitcast.9, s32[15,15]{1,0:T(8,128)} %keep_in.1, s32[1,15]{1,0:T(1,128)} %bitcast.12), custom_call_target="tpu_custom_call" | custom-call | tf_op jit(solution)/shard_map/square/pallas_call | solution.py:546
  63.6 1.3 %copy.11 = bf16[120,40]{0,1:T(8,128)(2,1)} copy(bf16[120,40]{0,1:T(8,128)(2,1)} %bitcast.11) | data formatting | bytes 19200

commit v5 on v4

--- a/solution.py
+++ b/solution.py
@@ -18,7 +18,7 @@
 OUT = 40
 KWIN = 1152
 PART = 272
-EARLY = 3
+EARLY = 2
 STEPS = 14
 LAST = COLS - 3 * TILE
 SPARE = TILE - LAST
@@ -63,8 +63,8 @@
 
 def kernel(
     row_in, col_in, win_in, stripe_in, ctab_in, keep_in, branch_in,
-    out_ref, occ_ref,
-    row_ref, col_ref, win_ref, stripe_ref, ctab_ref, keep_ref, branch_ref, in_sem,
+    out, occ_out,
+    row_ref, col_ref, win_ref, stripe_ref, ctab_ref, keep_ref, branch_ref, in_sem, out_ref, occ_ref, out_sem,
     rm, rb, lg, acc, ct, zin, occx, occy, occc, occz, keepm, branchm, um,
     rsend, rrecv, go, dsend, drecv, own_sem, lsend, lrecv, lsibs, lsibr, zsend, zrecv, osend, orecv,
 ):
@@ -405,12 +405,12 @@
 
     points = (
         dict(
-            la=(0, 2), o1=(0, 5), lb=(0, 7), o2=(0, 9), lf=(1, 3), m0a=(0, 12), m0b=(0, 13), m0c=(1, 4),
-            m0d=(1, 5), m1a=(1, 8), m1b=(1, 9), m1c=(1, 10), m1d=(1, 11), end=(1, 13),
+            la=(0, 2), o1=(0, 5), lb=(0, 7), o2=(0, 9), lf=(1, 3), m0a=(0, 12), m0b=(0, 13), m0c=(0, 13),
+            m0d=(0, 13), m1a=(1, 8), m1b=(1, 9), m1c=(1, 10), m1d=(1, 11), end=(1, 13),
         ),
         dict(
-            la=(0, 2), o1=(0, 5), lb=(0, 7), o2=(0, 9), lf=(1, 2), m0a=(0, 12), m0b=(0, 13), m0c=(1, 3),
-            m0d=(1, 4), m1a=(1, 6), m1b=(1, 7), m1c=(1, 8), m1d=(1, 9), end=(1, 10),
+            la=(0, 2), o1=(0, 5), lb=(0, 7), o2=(0, 9), lf=(1, 2), m0a=(0, 12), m0b=(0, 13), m0c=(0, 13),
+            m0d=(1, 3), m1a=(1, 6), m1b=(1, 7), m1c=(1, 8), m1d=(1, 9), end=(1, 10),
         ),
     )
 
@@ -514,7 +514,9 @@
     for j in range(1, Z):
         whole = whole + occz[j]
     mean = jnp.sum(whole, keepdims=True) / float(ROWS * 2 * Y)
-    occ_ref[...] = mean
+    occ_ref[...] = jnp.broadcast_to(mean, (1, TILE))
+    occ_store = pltpu.make_async_copy(occ_ref, occ_out, out_sem.at[0])
+    occ_store.start()
 
     for d in ways:
         for k in range(3):
@@ -535,22 +537,25 @@
     doubled = 2.0 * win_ref[...].astype(jnp.float32) - square
     updated = jnp.where(branchm[...] > 0.5, doubled, square)
     out_ref[...] = jnp.where(keepm[...] > 0.5, updated, 0.0).astype(jnp.bfloat16)
+    out_store = pltpu.make_async_copy(out_ref, out, out_sem.at[1])
+    out_store.start()
     for t in range(2):
         scatter(t, False)
+    occ_store.wait()
+    out_store.wait()
 
 
 def shards(row_stripe, column_stripe, window_block, stripe_tiles, column_tiles, keep_tiles, branch):
     bf, f32 = jnp.bfloat16, jnp.float32
     dma = pltpu.SemaphoreType.DMA
-    vmem = pl.BlockSpec(memory_space=pltpu.VMEM)
     block, occupancy = pl.pallas_call(
         kernel,
         out_shape=(
             jax.ShapeDtypeStruct((OUT, ROWS), bf),
-            jax.ShapeDtypeStruct((1, 1), f32),
+            jax.ShapeDtypeStruct((1, TILE), f32),
         ),
         in_specs=[pl.BlockSpec(memory_space=pl.ANY)] * 7,
-        out_specs=(vmem, vmem),
+        out_specs=(pl.BlockSpec(memory_space=pl.ANY),) * 2,
         scratch_shapes=[
             pltpu.VMEM((ROWS, PANEL), bf),
             pltpu.VMEM((SUB, COLS), bf),
@@ -560,6 +565,9 @@
             pltpu.VMEM((15, 15), jnp.int32),
             pltpu.VMEM((1, 15), jnp.int32),
             dma((7,)),
+            pltpu.VMEM((OUT, ROWS), bf),
+            pltpu.VMEM((1, TILE), f32),
+            dma((2,)),
             pltpu.VMEM((4, SUB, TILE), bf),
             pltpu.VMEM((2, Y, KWIN, TILE), bf),
             pltpu.VMEM((X, 2 * ROWS_P, PANEL), bf),

time: 66.9 us -> 65.5 us (0.979)
  Pallas kernels: 63 us -> 62.2 us
    pallas_call x1, Pallas kernels: 63 us -> 62.2 us  [shards(): pl.pallas_call(kernel, out_shape=(jax.ShapeDtypeStruct((OUT, ROWS), bf),...]
where the time goes in v5:
time: 65.5 us; the launch traced here: 65.3 us
  Pallas kernels  62.2 us (95%)
  between operations  1.81 us (3%)
  local copies, waits for them, and re-layouts  1.31 us (2%)
    pallas_call x1, Pallas kernels, shards(): pl.pallas_call(kernel, out_shape=(jax.ShapeDtypeStruct((OUT, ROWS), bf),...  62.2 us

profile of v5, /device:TPU:1, one launch (start us, length us, event | category | flops | bytes accessed | tf_op | source)
XLA Modules:
  0.0 65.3 jit_solution(998482159452799151)
XLA Ops:
  0.6 62.2 %square.1 = (bf16[40,120]{1,0:T(8,128)(2,1)}, f32[1,128]{1,0:T(1,128)}) custom-call(bf16[120,2176]{1,0:T(8,128)(2,1)} %bitcast.9, bf16[544,480]{1,0:T(8,128)(2,1)} %bitcast.8, bf16[40,120]{1,0:T(8,128)(2,1)} %bitcast.11, s32[15,816]{1,0:T(8,128)} %stripe_in.1, s32[15,816]{1,0:T(8,128)} %bitcast.10, s32[15,15]{1,0:T(8,128)} %keep_in.1, s32[1,15]{1,0:T(1,128)} %bitcast.13), custom_call_target="tpu_custom_call" | custom-call | tf_op jit(solution)/shard_map/square/pallas_call | solution.py:551
  62.8 0.0 copy-start
  62.8 1.3 %copy.11 = bf16[120,40]{0,1:T(8,128)(2,1)} copy(bf16[120,40]{0,1:T(8,128)(2,1)} %bitcast.12) | data formatting | bytes 19200
  64.1 0.0 copy-done
Async XLA Ops:
  62.8 1.3 %copy-start = (f32[1,128]{1,0:T(1,128)S(1)}, f32[1,128]{1,0:T(1,128)}, u32[]{:S(2)}) copy-start(f32[1,128]{1,0:T(1,128)} %get-tuple-element.5) | copy-start | bytes 1540

commit v6 on v5

--- a/solution.py
+++ b/solution.py
@@ -87,9 +87,6 @@
         (keep_in, keep_ref), (branch_in, branch_ref), (win_in, win_ref),
     ]
     loads = [pltpu.make_async_copy(a, b, in_sem.at[i]) for i, (a, b) in enumerate(arrays)]
-    for load in loads:
-        load.start()
-
     barrier = pltpu.get_barrier_semaphore()
     plane = [((y + d) % Y * 2, x, z) for d in range(1, Y)] + [(y * 2, (x + d) % X, z) for d in range(1, X)]
     others = [(y * 2 + 1, x, (z + d) % Z) for d in range(1, Z)]
@@ -99,6 +96,9 @@
     @pl.when(c == 1)
     def _():
         pl.semaphore_signal(barrier, inc=1, device_id=sib, device_id_type=MESH)
+
+    for load in loads:
+        load.start()
 
     def agree(counter, count, i):
         @pl.when(c == counter)

time: 65.5 us -> 65.5 us (level)
  no operation moved by 1% of the time
where the time goes in v6:
time: 65.5 us; the launch traced here: 65.3 us
  Pallas kernels  62.2 us (95%)
  between operations  1.81 us (3%)
  local copies, waits for them, and re-layouts  1.31 us (2%)
    pallas_call x1, Pallas kernels, shards(): pl.pallas_call(kernel, out_shape=(jax.ShapeDtypeStruct((OUT, ROWS), bf),...  62.2 us

profile of v6, /device:TPU:1, one launch (start us, length us, event | category | flops | bytes accessed | tf_op | source)
XLA Modules:
  0.0 65.3 jit_solution(14798009438231332858)
XLA Ops:
  0.6 62.2 %square.1 = (bf16[40,120]{1,0:T(8,128)(2,1)}, f32[1,128]{1,0:T(1,128)}) custom-call(bf16[120,2176]{1,0:T(8,128)(2,1)} %bitcast.9, bf16[544,480]{1,0:T(8,128)(2,1)} %bitcast.8, bf16[40,120]{1,0:T(8,128)(2,1)} %bitcast.11, s32[15,816]{1,0:T(8,128)} %stripe_in.1, s32[15,816]{1,0:T(8,128)} %bitcast.10, s32[15,15]{1,0:T(8,128)} %keep_in.1, s32[1,15]{1,0:T(1,128)} %bitcast.13), custom_call_target="tpu_custom_call" | custom-call | tf_op jit(solution)/shard_map/square/pallas_call | solution.py:551
  62.8 0.0 copy-start
  62.8 1.3 %copy.11 = bf16[120,40]{0,1:T(8,128)(2,1)} copy(bf16[120,40]{0,1:T(8,128)(2,1)} %bitcast.12) | data formatting | bytes 19200
  64.1 0.0 copy-done
Async XLA Ops:
  62.8 1.3 %copy-start = (f32[1,128]{1,0:T(1,128)S(1)}, f32[1,128]{1,0:T(1,128)}, u32[]{:S(2)}) copy-start(f32[1,128]{1,0:T(1,128)} %get-tuple-element.5) | copy-start | bytes 1540
